TPU v7x, 32 devices: a whole 2x2x4 slice. The times are simulated.
32 devices in a mesh: seq: 8 (over y, x, core), exp: 4 (over z).
Axes of the slice: x: 2, y: 2, z: 4, core: 2. Of those that a mesh axis runs over, the one named last changes fastest.
Arguments:
- tokens: bfloat16 [2, 4096, 1024], P(None, 'seq'), may hold values from -48 to 48
- router: bfloat16 [1024, 512], P(None, 'exp'), may hold values from -4 to 4
- w_in: bfloat16 [32, 1024, 2048], P(('exp', 'seq')), may hold values from -0.1875 to 0.1875
- w_out: bfloat16 [32, 2048, 1024], P(('exp', 'seq')), may hold values from -0.125 to 0.125
Outputs:
- mixed: bfloat16 [2, 4096, 1024], P(None, ('seq', 'exp'))
All inputs are finite; a program needn't handle non-finite values.
Results may differ from a plain program's by a relative error of at most 0.015.
Values may be sent and summed in bfloat16 or wider, within the bound.
A program may use at most 64 MiB of HBM per device.

v0:
```python
import jax
import jax.numpy as jnp
from jax import lax
from jax.sharding import PartitionSpec as P

SLOTS = 16


def shards(tokens, router, w_in, w_out):
    local_columns = router.shape[1]
    local_experts = local_columns // SLOTS
    seq_count = tokens.shape[0]
    width = tokens.shape[2]
    router_logits = jnp.einsum("bnq,qt->bnt", tokens, router, preferred_element_type=jnp.float32)
    column_top = lax.pmax(jnp.max(router_logits, axis=1), "seq")
    column_sum = lax.psum(jnp.sum(jnp.exp(router_logits - column_top[:, None, :]), axis=1), "seq")
    dispatch_weights = (
        jnp.exp(router_logits - column_top[:, None, :]) / column_sum[:, None, :]
    ).astype(jnp.bfloat16)
    partial_slot_sums = jnp.einsum(
        "mja,mjo->mao", dispatch_weights, tokens, preferred_element_type=jnp.float32
    )
    slot_input_rows = lax.psum(partial_slot_sums, "seq").astype(jnp.bfloat16)
    split_count = lax.axis_size("seq") // local_experts
    own_expert = lax.axis_index("seq") // split_count
    own_input = lax.dynamic_slice_in_dim(slot_input_rows, own_expert * SLOTS, SLOTS, 1).reshape(
        seq_count * SLOTS, width
    )
    pre_active = jnp.dot(own_input, w_in[0], preferred_element_type=jnp.float32)
    hidden = jax.nn.gelu(pre_active, approximate=True).astype(jnp.bfloat16)
    piece_output = jnp.dot(hidden, w_out[0], preferred_element_type=jnp.float32).reshape(
        seq_count, 1, SLOTS, width
    )
    expert_mask = (jnp.arange(local_experts, dtype=jnp.int32) == own_expert).astype(jnp.float32)
    placed = (piece_output * expert_mask[None, :, None, None]).reshape(
        seq_count, local_columns, width
    )
    slot_output_rows = lax.psum(placed, "seq").astype(jnp.bfloat16)
    router_all = lax.all_gather(router, "exp", axis=1, tiled=True)
    row_count = tokens.shape[1] // lax.axis_size("exp")
    first_row = lax.axis_index("exp") * row_count
    own_tokens = lax.dynamic_slice_in_dim(tokens, first_row, row_count, 1)
    row_scores = jnp.einsum(
        "bnq,qt->bnt", own_tokens, router_all, preferred_element_type=jnp.float32
    )
    row_top = jnp.max(row_scores, axis=2, keepdims=True)
    row_exp = jnp.exp(row_scores - row_top)
    combine_weights = (row_exp / jnp.sum(row_exp, axis=2, keepdims=True)).astype(jnp.bfloat16)
    mixed = jnp.einsum(
        "ptx,pxg->ptg",
        combine_weights,
        lax.all_gather(slot_output_rows, "exp", axis=1, tiled=True),
        preferred_element_type=jnp.float32,
    )
    return mixed.astype(jnp.bfloat16)


def solution(mesh):
    placed = (
        P(None, "seq", None),
        P(None, "exp"),
        P(("exp", "seq"), None, None),
        P(("exp", "seq"), None, None),
    )
    return jax.shard_map(
        shards, mesh=mesh, in_specs=placed, out_specs=P(None, ("seq", "exp"), None), check_vma=False
    )
```

profile of v0, /device:TPU:0, one launch (start us, length us, event | category | flops | bytes accessed | tf_op | source)
XLA Modules:
  0.0 201.8 jit_solution(17430647817749464838)
XLA Ops:
  6.5 0.0 copy-start
  6.5 0.0 all-gather.3.cloned.1.call-start
  6.5 0.7 all-gather.3.cloned.1.call-update
  7.3 0.0 all-gather.5.cloned.1.call-start
  7.3 0.8 copy-done
  8.1 1.7 fusion.31
  9.8 15.1 %pmax.7 = f32[2,128]{1,0:T(2,128)S(1)} all-reduce(f32[2,128]{1,0:T(2,128)S(1)} %get-tuple-element.5), channel_id=1, replica_groups=mesh['seq'=8,'exp'=4] {'seq'}, use_global_device_ids=true, to_apply=%region_3.0 | all-reduce | flops 256 | bytes 2048 | tf_op jit(solution)/shard_map/pmax | solution.py:15
  24.9 0.1 fusion.10
  25.0 12.6 %psum.21 = f32[2,128]{1,0:T(2,128)S(1)} all-reduce(f32[2,128]{1,0:T(2,128)S(1)} %fusion.10), channel_id=1, replica_groups=mesh['seq'=8,'exp'=4] {'seq'}, use_global_device_ids=true, to_apply=%region_5.6 | all-reduce | flops 256 | bytes 2048 | tf_op jit(solution)/shard_map/psum | solution.py:16
  37.6 1.5 fusion.23
  39.1 0.1 mul.58
  39.2 0.1 mul.59
  39.3 50.5 %all-reduce.2 = bf16[2,128,1024]{2,1,0:T(8,128)(2,1)S(1)} all-reduce(f32[2,128,1024]{2,1,0:T(8,128)} %fusion.23), channel_id=1, replica_groups=mesh['seq'=8,'exp'=4] {'seq'}, use_global_device_ids=true, to_apply=%region_6.7 | all-reduce | flops 262144 | bytes 1572864 | tf_op jit(solution)/shard_map/psum | solution.py:23
  89.8 0.0 copy-start.1
  89.8 3.2 %fusion.20 = bf16[32,2048]{1,0:T(8,128)(2,1)S(1)} fusion(bf16[32,1024]{1,0:T(8,128)(2,1)S(1)} %bitcast.31, bf16[1,1024,2048]{2,1,0:T(8,128)(2,1)} %param.6), kind=kOutput, calls=%fused_computation.24 | convolution fusion | flops 134807552 | bytes 4390912 | tf_op jit(solution)/shard_map/dot_general | solution.py:29
  93.0 0.2 copy-done.1
  93.2 0.8 fusion.1
  94.1 0.1 bitcast_multiply_fusion
  94.2 50.7 %all-reduce.3 = bf16[2,128,1024]{2,1,0:T(8,128)(2,1)} all-reduce(f32[2,128,1024]{2,1,0:T(8,128)S(1)} %bitcast_multiply_fusion), channel_id=1, replica_groups=mesh['seq'=8,'exp'=4] {'seq'}, use_global_device_ids=true, to_apply=%region_7.8 | all-reduce | flops 262144 | bytes 1572864 | tf_op jit(solution)/shard_map/psum | solution.py:38
  145.0 0.0 all-gather.5.cloned.1.call-update
  145.0 0.0 all-gather.3.cloned.1.call-done
  145.0 1.7 fusion.7
  146.7 0.2 fusion.32
  146.9 45.0 %all-gather.5.cloned.1.call-done = bf16[2,512,1024]{2,1,0:T(8,128)(2,1)} async-done(((bf16[2,128,1024]{2,1,0:T(8,128)(2,1)}), bf16[2,512,1024]{2,1,0:T(8,128)(2,1)}) %all-gather.5.cloned.1.call-update) | async-done | bytes 2097168 | tf_op jit(solution)/shard_map/all_gather | solution.py:52
  191.9 3.0 %convolution_convert_fusion = bf16[2,128,1024]{2,1,0:T(8,128)(2,1)} fusion(bf16[2,512,1024]{2,1,0:T(8,128)(2,1)} %all-gather.5.cloned.1.call-done, f32[2,128]{1,0:T(2,128)S(1)} %fusion.32, f32[2,128,512]{2,1,0:T(8,128)S(1)} %fusion.7), kind=kOutput, calls=%fused_computation.5 | convolution fusion | flops 269091584 | bytes 3146752 | tf_op jit(solution)/shard_map/ptx,pxg->ptg/dot_general | solution.py:49
  (2 shorter events, 0.0 us)
Async XLA Ops:
  6.5 1.6 copy-start
  6.5 138.5 %all-gather.3.cloned.1.call-start = ((), (), s32[]{:S(2)}) async-start(), calls=%async_computation | async-start | bytes 1310720 | tf_op jit(solution)/shard_map/all_gather | solution.py:39
  7.3 184.6 %all-gather.5.cloned.1.call-start = ((), (), s32[]{:S(2)}) async-start(), calls=%async_computation.1 | async-start | bytes 2621440 | tf_op jit(solution)/shard_map/all_gather | solution.py:52
  89.8 3.5 %copy-start.1 = (bf16[1,2048,1024]{2,1,0:T(8,128)(2,1)S(1)}, bf16[1,2048,1024]{2,1,0:T(8,128)(2,1)}, u32[]{:S(2)}) copy-start(bf16[1,2048,1024]{2,1,0:T(8,128)(2,1)} %param.7) | copy-start | bytes 12582916
Sparse Core Ops, SparseCore 0:
  8.9 32.8 all-gather.2
  145.1 46.7 all-gather.4
where the time goes:
time: 202 us
  blocking collectives  129 us (64%)
  waiting for transfers between devices  45.7 us (23%)
  between operations  13.5 us (7%)
  matrix products  11.9 us (6%)
    psum x1, blocking collectives, shards(): slot_output_rows = lax.psum(placed, 'seq').astype(jnp.bfloat16)  50.7 us
    psum x1, blocking collectives, shards(): slot_input_rows = lax.psum(partial_slot_sums, 'seq').astype(jnp.bfloat16)  50.5 us
    all_gather x1, waiting for transfers between devices, shards(): lax.all_gather(slot_output_rows, 'exp', axis=1, tiled=True)  45 us
    pmax x1, blocking collectives, shards(): column_top = lax.pmax(jnp.max(router_logits, axis=1), 'seq')  15.1 us
    psum x1, blocking collectives, shards(): lax.psum(jnp.sum(jnp.exp(router_logits - column_top[:, None, :]), axis=1)...  12.6 us
  transfers between devices with their start and end apart: 2, of which 1 were waited for; matrix products, arithmetic and copies ran while one was open for 5% of the time, Pallas kernels for 0%

commit v1 on v0

v1 whole, which is shorter than its diff:
```python
import functools

import jax
import jax.numpy as jnp
from jax import lax
from jax.experimental import pallas as pl
from jax.experimental.pallas import tpu as pltpu
from jax.sharding import PartitionSpec as P

SLOTS = 16
MESH = pl.DeviceIdType.MESH
F32 = jnp.float32
BF16 = jnp.bfloat16


def flip(index, mask):
    bit = 1
    while bit <= mask:
        if mask & bit:
            index = index + bit - 2 * bit * ((index // bit) % 2)
        bit *= 2
    return index


def partner(index, step, count):
    if count & (count - 1) == 0:
        return flip(index, step)
    return (index + step) % count


def layer(
    n_seq, n_exp,
    tokens_ref, router_ref, w_in_ref, w_out_ref, mixed_ref,
    tok, routers, w1, w2, psend, precv, ssend, srecv, coef, x_ref, pout, xrecv, slots, comb, inv,
    load_sem, rz_send, rz_recv, rs_send, rs_recv, p_send, p_recv, s_send, s_recv,
    q_send, q_recv, z_send, z_recv, c_send, c_recv, b_send, b_recv,
):
    seqs, length, width = tok.shape
    cols = router_ref.shape[1]
    hidden = w1.shape[1]
    experts = cols // SLOTS
    split = n_seq // experts
    chips = n_seq // 2
    rows = length // n_exp
    half = width // 2

    me_s = lax.axis_index("seq")
    me_e = lax.axis_index("exp")
    core = me_s % 2
    chip = me_s // 2
    sib = me_s + 1 - 2 * core
    own = me_s // split
    me_q = me_s % split

    loads = [
        pltpu.make_async_copy(router_ref, routers.at[me_e], load_sem.at[0]),
        pltpu.make_async_copy(tokens_ref, tok, load_sem.at[1]),
        pltpu.make_async_copy(w_in_ref.at[0], w1, load_sem.at[2]),
        pltpu.make_async_copy(w_out_ref.at[0], w2, load_sem.at[3]),
    ]
    for load in loads:
        load.start()

    barrier = pltpu.get_barrier_semaphore()
    for k in range(1, n_seq):
        pl.semaphore_signal(barrier, inc=1, device_id=(partner(me_s, k, n_seq), me_e), device_id_type=MESH)
    for k in range(1, n_exp):
        pl.semaphore_signal(barrier, inc=1, device_id=(me_s, partner(me_e, k, n_exp)), device_id_type=MESH)
    pl.semaphore_wait(barrier, n_seq + n_exp - 2)

    def remote(src, dst, send, recv, seq, exp):
        return pltpu.make_async_remote_copy(
            src_ref=src, dst_ref=dst, send_sem=send, recv_sem=recv,
            device_id=(seq, exp), device_id_type=MESH,
        )

    started = []

    def router_half(owner, which):
        return routers.at[owner, pl.ds(pl.multiple_of(which * half, half), half), :]

    loads[0].wait()
    for k in range(1, n_exp):
        other = partner(me_e, k, n_exp)
        piece = router_half(me_e, core)
        copy = remote(piece, piece, rz_send.at[k], rz_recv.at[k], me_s, other)
        copy.start()
        started.append(copy)

    loads[1].wait()
    ssend[...] = jnp.zeros_like(ssend)
    for s in range(seqs):
        score = jnp.dot(tok[s], routers[me_e], preferred_element_type=F32)
        top = jnp.max(score, axis=0, keepdims=True)
        weight = jnp.exp(score - top)
        ssend[s : s + 1, :] = top
        ssend[seqs + s : seqs + s + 1, :] = jnp.sum(weight, axis=0, keepdims=True)
        psend[s] = jnp.dot(weight.T.astype(BF16), tok[s], preferred_element_type=F32).astype(BF16)

    def slot_rows(expert):
        return pl.ds(pl.multiple_of(expert * SLOTS, SLOTS), SLOTS)

    for k in range(1, n_seq):
        other = partner(me_s, k, n_seq)
        for copy in (
            remote(ssend, srecv.at[me_s], s_send.at[k], s_recv.at[k], other, me_e),
            remote(psend.at[:, slot_rows(other // split), :], precv.at[me_s], p_send.at[k], p_recv.at[k], other, me_e),
        ):
            copy.start()
            started.append(copy)
    srecv[me_s] = ssend[...]
    precv[me_s] = psend[:, slot_rows(own), :]

    for k in range(1, n_exp):
        other = partner(me_e, k, n_exp)
        piece = router_half(other, core)
        remote(piece, piece, rz_send.at[k], rz_recv.at[k], me_s, other).wait_recv()
        copy = remote(piece, piece, rs_send.at[k], rs_recv.at[k], sib, me_e)
        copy.start()
        started.append(copy)
    for k in range(1, n_exp):
        piece = router_half(partner(me_e, k, n_exp), 1 - core)
        remote(piece, piece, rs_send.at[k], rs_recv.at[k], sib, me_e).wait_recv()
    for s in range(seqs):
        mine = tok[s, pl.ds(pl.multiple_of(me_e * rows, rows), rows), :]
        score = jnp.concatenate(
            [jnp.dot(mine, routers[e], preferred_element_type=F32) for e in range(n_exp)], axis=1
        )
        weight = jnp.exp(score - jnp.max(score, axis=1, keepdims=True))
        inv[s] = jnp.broadcast_to(1.0 / jnp.sum(weight, axis=1, keepdims=True), (rows, 128))
        comb[s] = weight.astype(BF16)

    for k in range(1, n_seq):
        other = partner(me_s, k, n_seq)
        remote(ssend, srecv.at[other], s_send.at[k], s_recv.at[k], other, me_e).wait_recv()
    parts = []
    for s in range(seqs):
        top = srecv[:, s, :]
        scale = jnp.exp(top - jnp.max(top, axis=0, keepdims=True))
        total = jnp.sum(scale * srecv[:, seqs + s, :], axis=0, keepdims=True)
        parts.append(scale / total)
    fill = coef.shape[1] - seqs * n_seq
    if fill:
        parts.append(jnp.zeros((fill, cols), F32))
    coef[...] = jnp.concatenate(parts, axis=0).T
    factor = coef[slot_rows(own), :]
    for k in range(1, n_seq):
        other = partner(me_s, k, n_seq)
        remote(psend.at[:, slot_rows(own), :], precv.at[other], p_send.at[k], p_recv.at[k], other, me_e).wait_recv()
    for s in range(seqs):
        total = jnp.zeros((SLOTS, width), F32)
        for i in range(n_seq):
            at = s * n_seq + i
            total = total + factor[:, at : at + 1] * precv[i, s].astype(F32)
        x_ref[s * SLOTS : (s + 1) * SLOTS, :] = total.astype(BF16)

    loads[2].wait()
    loads[3].wait()
    x = x_ref[...]
    block = min(512, hidden)
    result = jnp.zeros((seqs * SLOTS, width), F32)
    for at in range(0, hidden, block):
        pre = jnp.dot(x, w1[:, at : at + block], preferred_element_type=F32)
        act = jax.nn.gelu(pre, approximate=True).astype(BF16)
        result = result + jnp.dot(act, w2[at : at + block, :], preferred_element_type=F32)

    def place(exp, seq):
        return slots.at[seq % split, :, slot_rows(exp * experts + seq // split), :]

    part = width // split
    if split == 1:
        slots[0, :, slot_rows(me_e * experts + own), :] = result.reshape(seqs, SLOTS, width).astype(BF16)
    else:
        for q in range(split):
            pout[q] = result[:, q * part : (q + 1) * part].reshape(seqs, SLOTS, part).astype(BF16)
        for k in range(1, split):
            other = (me_q + k) % split
            copy = remote(pout.at[other], xrecv.at[k], q_send.at[k], q_recv.at[k], me_s - me_q + other, me_e)
            copy.start()
            started.append(copy)
        total = pout[me_q].astype(F32)
        for k in range(1, split):
            remote(pout.at[me_q], xrecv.at[k], q_send.at[k], q_recv.at[k], me_s, me_e).wait_recv()
            total = total + xrecv[k].astype(F32)
        slots[me_q, :, slot_rows(me_e * experts + own), :] = total.astype(BF16)

    for k in range(1, n_exp):
        piece = place(me_e, me_s)
        copy = remote(piece, piece, z_send.at[k], z_recv.at[k], me_s, partner(me_e, k, n_exp))
        copy.start()
        started.append(copy)
    for j in range(n_exp):
        exp = partner(me_e, j, n_exp) if j else me_e
        piece = place(exp, me_s)
        if j:
            remote(piece, piece, z_send.at[j], z_recv.at[j], me_s, exp).wait_recv()
        for k in range(1, chips):
            copy = remote(piece, piece, c_send.at[j, k], c_recv.at[j, k], partner(chip, k, chips) * 2 + core, me_e)
            copy.start()
            started.append(copy)
        copy = remote(piece, piece, b_send.at[j, 0], b_recv.at[j, 0], sib, me_e)
        copy.start()
        started.append(copy)
    for j in range(n_exp):
        exp = partner(me_e, j, n_exp) if j else me_e
        for k in range(1, chips):
            seq = partner(chip, k, chips) * 2 + core
            piece = place(exp, seq)
            remote(piece, piece, c_send.at[j, k], c_recv.at[j, k], seq, me_e).wait_recv()
            copy = remote(piece, piece, b_send.at[j, k], b_recv.at[j, k], sib, me_e)
            copy.start()
            started.append(copy)
    for j in range(n_exp):
        exp = partner(me_e, j, n_exp) if j else me_e
        for k in range(chips):
            seq = (partner(chip, k, chips) if k else chip) * 2 + 1 - core
            piece = place(exp, seq)
            remote(piece, piece, b_send.at[j, k], b_recv.at[j, k], sib, me_e).wait_recv()

    for s in range(seqs):
        scale = inv[s][:, 0:1]
        for q in range(split):
            mix = jnp.dot(comb[s], slots[q, s], preferred_element_type=F32) * scale
            mixed_ref[s, :, q * part : (q + 1) * part] = mix.astype(BF16)

    for copy in started:
        copy.wait_send()


def shards(n_seq, n_exp, tokens, router, w_in, w_out):
    seqs, length, width = tokens.shape
    cols = router.shape[1]
    hidden = w_in.shape[2]
    experts = cols // SLOTS
    split = n_seq // experts
    chips = n_seq // 2
    rows = length // n_exp
    part = width // split
    stat_rows = -(-2 * seqs // 8) * 8
    lanes = -(-seqs * n_seq // 128) * 128
    dma = pltpu.SemaphoreType.DMA
    return pl.pallas_call(
        functools.partial(layer, n_seq, n_exp),
        out_shape=jax.ShapeDtypeStruct((seqs, rows, width), BF16),
        in_specs=[pl.BlockSpec(memory_space=pl.ANY)] * 4,
        out_specs=pl.BlockSpec(memory_space=pltpu.VMEM),
        scratch_shapes=[
            pltpu.VMEM((seqs, length, width), BF16),
            pltpu.VMEM((n_exp, width, cols), BF16),
            pltpu.VMEM((width, hidden), BF16),
            pltpu.VMEM((hidden, width), BF16),
            pltpu.VMEM((seqs, cols, width), BF16),
            pltpu.VMEM((n_seq, seqs, SLOTS, width), BF16),
            pltpu.VMEM((stat_rows, cols), F32),
            pltpu.VMEM((n_seq, stat_rows, cols), F32),
            pltpu.VMEM((cols, lanes), F32),
            pltpu.VMEM((seqs * SLOTS, width), BF16),
            pltpu.VMEM((split, seqs, SLOTS, part), BF16),
            pltpu.VMEM((split, seqs, SLOTS, part), BF16),
            pltpu.VMEM((split, seqs, n_exp * cols, part), BF16),
            pltpu.VMEM((seqs, rows, n_exp * cols), BF16),
            pltpu.VMEM((seqs, rows, 128), F32),
            dma((4,)),
            dma((n_exp,)), dma((n_exp,)), dma((n_exp,)), dma((n_exp,)),
            dma((n_seq,)), dma((n_seq,)), dma((n_seq,)), dma((n_seq,)),
            dma((split,)), dma((split,)),
            dma((n_exp,)), dma((n_exp,)),
            dma((n_exp, chips)), dma((n_exp, chips)),
            dma((n_exp, chips)), dma((n_exp, chips)),
        ],
        compiler_params=pltpu.CompilerParams(
            collective_id=0, has_side_effects=True, vmem_limit_bytes=56 * 1024 * 1024
        ),
    )(tokens, router, w_in, w_out)


def solution(mesh):
    placed = (
        P(None, "seq", None),
        P(None, "exp"),
        P(("exp", "seq"), None, None),
        P(("exp", "seq"), None, None),
    )
    return jax.shard_map(
        functools.partial(shards, mesh.shape["seq"], mesh.shape["exp"]),
        mesh=mesh, in_specs=placed, out_specs=P(None, ("seq", "exp"), None), check_vma=False,
    )
```

time: 202 us -> 42.8 us (0.21)
  blocking collectives: 129 us -> 0 us
  waiting for transfers between devices: 45.7 us -> 0 us
  Pallas kernels: 0 us -> 40.1 us
  between operations: 13.5 us -> 0.01 us
  matrix products: 11.9 us -> 0 us
    psum x3 -> x0, blocking collectives: 114 us -> none  [the longest x1 50.7 us: shards(): slot_output_rows = lax.psum(placed, 'seq').astype(jnp.bfloat16)]
    all_gather x2 -> x0, waiting for transfers between devices: 45 us -> none  [the longest x1 45 us: shards(): lax.all_gather(slot_output_rows, 'exp', axis=1, tiled=True)]
    pallas_call x0 -> x1, Pallas kernels: none -> 40.1 us  [shards(): pl.pallas_call(functools.partial(layer, n_seq, n_exp), out_shape=jax.Shap...]
    pmax x1 -> x0, blocking collectives: 15.1 us -> none  [shards(): column_top = lax.pmax(jnp.max(router_logits, axis=1), 'seq')]
    dot_general x6 -> x0, matrix products: 11.9 us -> none  [the longest x1 3.21 us: shards(): pre_active = jnp.dot(own_input, w_in[0], preferred_element_type=jnp.float32)]
  transfers between devices with their start and end apart: 2 -> 0, of which waited for: 1 -> 0; matrix products, arithmetic and copies ran while one was open for 5% -> 0% of each run, Pallas kernels for 0% -> 0%
where the time goes in v1:
time: 42.8 us; the launch traced here: 42 us
  Pallas kernels  40.1 us (94%)
  local copies, waits for them, and re-layouts  1.87 us (4%)
    pallas_call x1, Pallas kernels, shards(): pl.pallas_call(functools.partial(layer, n_seq, n_exp), out_shape=jax.Shap...  40.1 us
    unnamed x1, local copies, waits for them, and re-layouts  1.87 us

profile of v1, /device:TPU:0, one launch (start us, length us, event | category | flops | bytes accessed | tf_op | source)
XLA Modules:
  0.0 42.0 jit_solution(6954738969507847531)
XLA Ops:
  0.0 40.1 %shard_map.46 = bf16[2,128,1024]{2,1,0:T(8,128)(2,1)} custom-call(bf16[2,512,1024]{2,1,0:T(8,128)(2,1)} %tokens_ref.1, bf16[1024,128]{1,0:T(8,128)(2,1)} %router_ref.1, bf16[1,1024,2048]{2,1,0:T(8,128)(2,1)} %w_in_ref.1, bf16[1,2048,1024]{2,1,0:T(8,128)(2,1)} %w_out_ref.1), custom_call_target="tpu_custom_call" | custom-call | tf_op jit(solution)/shard_map/pallas_call | solution.py:242
  40.1 1.9 %copy.6 = bf16[2,128,1024]{2,1,0:T(8,128)(2,1)} copy(bf16[2,128,1024]{2,1,0:T(8,128)(2,1)} %shard_map.46) | data formatting | bytes 1048576

commit v2 on v1

--- a/solution.py
+++ b/solution.py
@@ -28,12 +28,27 @@
     return (index + step) % count
 
 
+def grid_of(chips):
+    cols = 1
+    while cols * cols * 4 <= chips and chips % (cols * 2) == 0:
+        cols *= 2
+    return chips // cols, cols
+
+
+def loop(start, stop, step):
+    if stop - start <= 4:
+        for j in range(start, stop):
+            step(j)
+    else:
+        pl.loop(start, stop)(step)
+
+
 def layer(
     n_seq, n_exp,
     tokens_ref, router_ref, w_in_ref, w_out_ref, mixed_ref,
     tok, routers, w1, w2, psend, precv, ssend, srecv, coef, x_ref, pout, xrecv, slots, comb, inv,
     load_sem, rz_send, rz_recv, rs_send, rs_recv, p_send, p_recv, s_send, s_recv,
-    q_send, q_recv, z_send, z_recv, c_send, c_recv, b_send, b_recv,
+    q_send, q_recv, z_send, z_recv, c_send, c_recv, d_send, d_recv, b_send, b_recv,
 ):
     seqs, length, width = tok.shape
     cols = router_ref.shape[1]
@@ -58,8 +73,8 @@
         pltpu.make_async_copy(w_in_ref.at[0], w1, load_sem.at[2]),
         pltpu.make_async_copy(w_out_ref.at[0], w2, load_sem.at[3]),
     ]
-    for load in loads:
-        load.start()
+    loads[0].start()
+    loads[1].start()
 
     barrier = pltpu.get_barrier_semaphore()
     for k in range(1, n_seq):
@@ -88,6 +103,8 @@
         started.append(copy)
 
     loads[1].wait()
+    loads[2].start()
+    loads[3].start()
     ssend[...] = jnp.zeros_like(ssend)
     for s in range(seqs):
         score = jnp.dot(tok[s], routers[me_e], preferred_element_type=F32)
@@ -110,25 +127,6 @@
             started.append(copy)
     srecv[me_s] = ssend[...]
     precv[me_s] = psend[:, slot_rows(own), :]
-
-    for k in range(1, n_exp):
-        other = partner(me_e, k, n_exp)
-        piece = router_half(other, core)
-        remote(piece, piece, rz_send.at[k], rz_recv.at[k], me_s, other).wait_recv()
-        copy = remote(piece, piece, rs_send.at[k], rs_recv.at[k], sib, me_e)
-        copy.start()
-        started.append(copy)
-    for k in range(1, n_exp):
-        piece = router_half(partner(me_e, k, n_exp), 1 - core)
-        remote(piece, piece, rs_send.at[k], rs_recv.at[k], sib, me_e).wait_recv()
-    for s in range(seqs):
-        mine = tok[s, pl.ds(pl.multiple_of(me_e * rows, rows), rows), :]
-        score = jnp.concatenate(
-            [jnp.dot(mine, routers[e], preferred_element_type=F32) for e in range(n_exp)], axis=1
-        )
-        weight = jnp.exp(score - jnp.max(score, axis=1, keepdims=True))
-        inv[s] = jnp.broadcast_to(1.0 / jnp.sum(weight, axis=1, keepdims=True), (rows, 128))
-        comb[s] = weight.astype(BF16)
 
     for k in range(1, n_seq):
         other = partner(me_s, k, n_seq)
@@ -154,6 +152,13 @@
             total = total + factor[:, at : at + 1] * precv[i, s].astype(F32)
         x_ref[s * SLOTS : (s + 1) * SLOTS, :] = total.astype(BF16)
 
+    for k in range(1, n_exp):
+        other = partner(me_e, k, n_exp)
+        piece = router_half(other, core)
+        remote(piece, piece, rz_send.at[k], rz_recv.at[k], me_s, other).wait_recv()
+        copy = remote(piece, piece, rs_send.at[k], rs_recv.at[k], sib, me_e)
+        copy.start()
+        started.append(copy)
     loads[2].wait()
     loads[3].wait()
     x = x_ref[...]
@@ -184,38 +189,177 @@
             total = total + xrecv[k].astype(F32)
         slots[me_q, :, slot_rows(me_e * experts + own), :] = total.astype(BF16)
 
+    grid_rows, grid_cols = grid_of(chips)
+    my_row = chip // grid_cols
+    my_col = chip % grid_cols
+
+    def peer(axis, k):
+        if axis == 0:
+            return partner(my_row, k, grid_rows) * grid_cols + my_col
+        return my_row * grid_cols + partner(my_col, k, grid_cols)
+
+    def corner(k0, k1):
+        return partner(my_row, k0, grid_rows) * grid_cols + partner(my_col, k1, grid_cols)
+
+    sizes = (grid_rows, grid_cols)
+    def one(exp, seq, s):
+        return slots.at[seq % split, s, slot_rows(exp * experts + seq // split), :]
+
+    far = (2 * me_e) // n_exp
+    inner = 2 * (me_e + far * (n_exp - 1 - 2 * me_e))
+
+    def nearest(j):
+        outer = -((inner - j) // (2 * n_exp))
+        sign = 2 * (j % 2) - 1
+        exp = (1 - outer) * (me_e + sign * ((j + 1) // 2)) + outer * (j + far * (n_exp - 1 - 2 * j))
+        return exp, outer * (2 * far - 1) - (1 - outer) * sign
+
+    def along(exp, way):
+        at, hops = (1 - way) // 2, way * (me_e - exp)
+        piece = place(exp, me_s)
+        return remote(piece, piece, z_send.at[at, hops], z_recv.at[at, hops + 1], me_s, me_e + way)
+
+    def arrival(exp, way):
+        at, hops = (1 - way) // 2, way * (me_e - exp)
+        piece = place(exp, me_s)
+        return remote(piece, piece, z_send.at[at, hops], z_recv.at[at, hops], me_s, me_e)
+
+    def inside(at):
+        return (at >= 0) & (at < n_exp)
+
+    def direct(exp, s, axis, k):
+        piece = one(exp, me_s, s)
+        return remote(piece, piece, c_send.at[exp, s, axis, k], c_recv.at[exp, s, axis, k], peer(axis, k) * 2 + core, me_e)
+
+    def direct_in(exp, s, axis, k):
+        piece = one(exp, peer(axis, k) * 2 + core, s)
+        return remote(piece, piece, c_send.at[exp, s, axis, k], c_recv.at[exp, s, axis, k], me_s, me_e)
+
+    def turned(exp, s, k0, k1):
+        first = s % 2
+        piece = one(exp, peer(first, k0) * 2 + core, s)
+        return remote(piece, piece, d_send.at[exp, s, k0, k1], d_recv.at[exp, s, k0, k1], peer(1 - first, k1) * 2 + core, me_e)
+
+    def turned_in(exp, s, k0, k1):
+        row, col = (k0, k1) if s % 2 == 0 else (k1, k0)
+        piece = one(exp, corner(row, col) * 2 + core, s)
+        return remote(piece, piece, d_send.at[exp, s, k0, k1], d_recv.at[exp, s, k0, k1], me_s, me_e)
+
+    def to_sibling(exp, row, col):
+        piece = place(exp, corner(row, col) * 2 + core)
+        return remote(piece, piece, b_send.at[exp, row, col], b_recv.at[exp, row, col], sib, me_e)
+
+    def from_sibling(exp, row, col):
+        piece = place(exp, corner(row, col) * 2 + 1 - core)
+        return remote(piece, piece, b_send.at[exp, row, col], b_recv.at[exp, row, col], sib, me_e)
+
+    def spread(exp):
+        for s in range(seqs):
+            for axis in (s % 2, 1 - s % 2):
+                for k in range(1, sizes[axis]):
+                    direct(exp, s, axis, k).start()
+        to_sibling(exp, 0, 0).start()
+
+    def turn(exp):
+        for s in range(seqs):
+            first = s % 2
+            for k0 in range(1, sizes[first]):
+                direct_in(exp, s, first, k0).wait_recv()
+                for k1 in range(1, sizes[1 - first]):
+                    turned(exp, s, k0, k1).start()
+
+    def share(exp):
+        for s in range(seqs):
+            second = 1 - s % 2
+            for k in range(1, sizes[second]):
+                direct_in(exp, s, second, k).wait_recv()
+        for row in range(grid_rows):
+            for col in range(grid_cols):
+                if row == 0 or col == 0:
+                    if row + col:
+                        to_sibling(exp, row, col).start()
+        for row in range(1, grid_rows):
+            for col in range(1, grid_cols):
+                for s in range(seqs):
+                    turned_in(exp, s, *((row, col) if s % 2 == 0 else (col, row))).wait_recv()
+                to_sibling(exp, row, col).start()
+
+    def finish(exp):
+        for row in range(grid_rows):
+            for col in range(grid_cols):
+                from_sibling(exp, row, col).wait_recv()
+                to_sibling(exp, row, col).wait_send()
+        for s in range(seqs):
+            first = s % 2
+            for axis in (0, 1):
+                for k in range(1, sizes[axis]):
+                    direct(exp, s, axis, k).wait_send()
+            for k0 in range(1, sizes[first]):
+                for k1 in range(1, sizes[1 - first]):
+                    turned(exp, s, k0, k1).wait_send()
+
+    for way in (1, -1):
+
+        @pl.when(inside(me_e + way))
+        def _():
+            along(me_e, way).start()
+
+    spread(me_e)
     for k in range(1, n_exp):
-        piece = place(me_e, me_s)
-        copy = remote(piece, piece, z_send.at[k], z_recv.at[k], me_s, partner(me_e, k, n_exp))
-        copy.start()
-        started.append(copy)
-    for j in range(n_exp):
-        exp = partner(me_e, j, n_exp) if j else me_e
-        piece = place(exp, me_s)
-        if j:
-            remote(piece, piece, z_send.at[j], z_recv.at[j], me_s, exp).wait_recv()
-        for k in range(1, chips):
-            copy = remote(piece, piece, c_send.at[j, k], c_recv.at[j, k], partner(chip, k, chips) * 2 + core, me_e)
-            copy.start()
-            started.append(copy)
-        copy = remote(piece, piece, b_send.at[j, 0], b_recv.at[j, 0], sib, me_e)
-        copy.start()
-        started.append(copy)
-    for j in range(n_exp):
-        exp = partner(me_e, j, n_exp) if j else me_e
-        for k in range(1, chips):
-            seq = partner(chip, k, chips) * 2 + core
-            piece = place(exp, seq)
-            remote(piece, piece, c_send.at[j, k], c_recv.at[j, k], seq, me_e).wait_recv()
-            copy = remote(piece, piece, b_send.at[j, k], b_recv.at[j, k], sib, me_e)
-            copy.start()
-            started.append(copy)
-    for j in range(n_exp):
-        exp = partner(me_e, j, n_exp) if j else me_e
-        for k in range(chips):
-            seq = (partner(chip, k, chips) if k else chip) * 2 + 1 - core
-            piece = place(exp, seq)
-            remote(piece, piece, b_send.at[j, k], b_recv.at[j, k], sib, me_e).wait_recv()
+        piece = router_half(partner(me_e, k, n_exp), 1 - core)
+        remote(piece, piece, rs_send.at[k], rs_recv.at[k], sib, me_e).wait_recv()
+    for s in range(seqs):
+        mine = tok[s, pl.ds(pl.multiple_of(me_e * rows, rows), rows), :]
+        score = jnp.concatenate(
+            [jnp.dot(mine, routers[e], preferred_element_type=F32) for e in range(n_exp)], axis=1
+        )
+        weight = jnp.exp(score - jnp.max(score, axis=1, keepdims=True))
+        inv[s] = jnp.broadcast_to(1.0 / jnp.sum(weight, axis=1, keepdims=True), (rows, 128))
+        comb[s] = weight.astype(BF16)
+
+
+    def pass_on(j):
+        exp, way = nearest(j)
+        arrival(exp, way).wait_recv()
+
+        @pl.when(inside(me_e + way))
+        def _():
+            along(exp, way).start()
+
+        spread(exp)
+
+    def step(j):
+        pass_on(j)
+        turn(nearest(j - 1)[0])
+
+        if isinstance(j, int):
+            if j >= 2:
+                share(nearest(j - 2)[0])
+        else:
+
+            @pl.when(j >= 2)
+            def _():
+                share(nearest(j - 2)[0])
+
+    loop(1, n_exp, step)
+    turn(nearest(n_exp - 1)[0])
+    loop(max(n_exp - 2, 0), n_exp, lambda j: share(nearest(j)[0]))
+
+    for way in (1, -1):
+
+        @pl.when(inside(me_e + way))
+        def _():
+            along(me_e, way).wait_send()
+
+    def end(j):
+        exp, way = nearest(j)
+
+        @pl.when(inside(me_e + way))
+        def _():
+            along(exp, way).wait_send()
+
+    loop(1, n_exp, end)
+    loop(0, n_exp, finish)
 
     for s in range(seqs):
         scale = inv[s][:, 0:1]
@@ -237,6 +381,7 @@
     rows = length // n_exp
     part = width // split
     stat_rows = -(-2 * seqs // 8) * 8
+    side = max(grid_of(chips))
     lanes = -(-seqs * n_seq // 128) * 128
     dma = pltpu.SemaphoreType.DMA
     return pl.pallas_call(
@@ -264,9 +409,10 @@
             dma((n_exp,)), dma((n_exp,)), dma((n_exp,)), dma((n_exp,)),
             dma((n_seq,)), dma((n_seq,)), dma((n_seq,)), dma((n_seq,)),
             dma((split,)), dma((split,)),
-            dma((n_exp,)), dma((n_exp,)),
-            dma((n_exp, chips)), dma((n_exp, chips)),
-            dma((n_exp, chips)), dma((n_exp, chips)),
+            dma((2, n_exp)), dma((2, n_exp)),
+            dma((n_exp, seqs, 2, side)), dma((n_exp, seqs, 2, side)),
+            dma((n_exp, seqs, side, side)), dma((n_exp, seqs, side, side)),
+            dma((n_exp, *grid_of(chips))), dma((n_exp, *grid_of(chips))),
         ],
         compiler_params=pltpu.CompilerParams(
             collective_id=0, has_side_effects=True, vmem_limit_bytes=56 * 1024 * 1024

time: 42.8 us -> 43.7 us (1.021); the launches traced: 42 us -> 43.5 us
  Pallas kernels: 40.1 us -> 41.7 us
    pallas_call x1, Pallas kernels: 40.1 us -> 41.7 us  [shards(): pl.pallas_call(functools.partial(layer, n_seq, n_exp), out_shape=jax.Shap...]
where the time goes in v2:
time: 43.7 us; the launch traced here: 43.5 us
  Pallas kernels  41.7 us (95%)
  local copies, waits for them, and re-layouts  1.87 us (4%)
    pallas_call x1, Pallas kernels, shards(): pl.pallas_call(functools.partial(layer, n_seq, n_exp), out_shape=jax.Shap...  41.7 us
    unnamed x1, local copies, waits for them, and re-layouts  1.87 us

profile of v2, /device:TPU:0, one launch (start us, length us, event | category | flops | bytes accessed | tf_op | source)
XLA Modules:
  0.0 43.5 jit_solution(9404313173304309389)
XLA Ops:
  0.0 41.7 %shard_map.46 = bf16[2,128,1024]{2,1,0:T(8,128)(2,1)} custom-call(bf16[2,512,1024]{2,1,0:T(8,128)(2,1)} %tokens_ref.1, bf16[1024,128]{1,0:T(8,128)(2,1)} %router_ref.1, bf16[1,1024,2048]{2,1,0:T(8,128)(2,1)} %w_in_ref.1, bf16[1,2048,1024]{2,1,0:T(8,128)(2,1)} %w_out_ref.1), custom_call_target="tpu_custom_call" | custom-call | tf_op jit(solution)/shard_map/pallas_call | solution.py:387
  41.7 1.9 %copy.6 = bf16[2,128,1024]{2,1,0:T(8,128)(2,1)} copy(bf16[2,128,1024]{2,1,0:T(8,128)(2,1)} %shard_map.46) | data formatting | bytes 1048576

commit v3 on v1

--- a/solution.py
+++ b/solution.py
@@ -31,7 +31,7 @@
 def layer(
     n_seq, n_exp,
     tokens_ref, router_ref, w_in_ref, w_out_ref, mixed_ref,
-    tok, routers, w1, w2, psend, precv, ssend, srecv, coef, x_ref, pout, xrecv, slots, comb, inv,
+    tok, routers, w1, w2, psend, precv, ssend, srecv, coef, x_ref, pout, xrecv, slots, comb, inv, perm,
     load_sem, rz_send, rz_recv, rs_send, rs_recv, p_send, p_recv, s_send, s_recv,
     q_send, q_recv, z_send, z_recv, c_send, c_recv, b_send, b_recv,
 ):
@@ -53,13 +53,13 @@
     me_q = me_s % split
 
     loads = [
-        pltpu.make_async_copy(router_ref, routers.at[me_e], load_sem.at[0]),
+        pltpu.make_async_copy(router_ref, routers.at[0], load_sem.at[0]),
         pltpu.make_async_copy(tokens_ref, tok, load_sem.at[1]),
         pltpu.make_async_copy(w_in_ref.at[0], w1, load_sem.at[2]),
         pltpu.make_async_copy(w_out_ref.at[0], w2, load_sem.at[3]),
     ]
-    for load in loads:
-        load.start()
+    loads[0].start()
+    loads[1].start()
 
     barrier = pltpu.get_barrier_semaphore()
     for k in range(1, n_seq):
@@ -76,21 +76,39 @@
 
     started = []
 
-    def router_half(owner, which):
-        return routers.at[owner, pl.ds(pl.multiple_of(which * half, half), half), :]
+    def router_half(k, which):
+        return routers.at[k, pl.ds(pl.multiple_of(which * half, half), half), :]
+
+    def router_over(k):
+        return remote(
+            router_half(0, core), router_half(k, core), rz_send.at[k], rz_recv.at[k], me_s, partner(me_e, k, n_exp)
+        )
+
+    def router_share(k, which):
+        piece = router_half(k, which)
+        return remote(piece, piece, rs_send.at[k], rs_recv.at[k], sib, me_e)
 
     loads[0].wait()
     for k in range(1, n_exp):
-        other = partner(me_e, k, n_exp)
-        piece = router_half(me_e, core)
-        copy = remote(piece, piece, rz_send.at[k], rz_recv.at[k], me_s, other)
-        copy.start()
-        started.append(copy)
+        router_over(k).start()
+        started.append(router_over(k))
+
+    if split == 1:
+        count = n_exp * cols
+        source = lax.broadcasted_iota(jnp.int32, (count, count), 0)
+        target = lax.broadcasted_iota(jnp.int32, (count, count), 1)
+        pair = 2 * SLOTS
+        wanted = (
+            (source // SLOTS) % 2 * (count // 2) + source // pair * SLOTS + source % SLOTS
+        )
+        perm[...] = (wanted == target).astype(F32).astype(BF16)
 
     loads[1].wait()
+    loads[2].start()
+    loads[3].start()
     ssend[...] = jnp.zeros_like(ssend)
     for s in range(seqs):
-        score = jnp.dot(tok[s], routers[me_e], preferred_element_type=F32)
+        score = jnp.dot(tok[s], routers[0], preferred_element_type=F32)
         top = jnp.max(score, axis=0, keepdims=True)
         weight = jnp.exp(score - top)
         ssend[s : s + 1, :] = top
@@ -110,25 +128,6 @@
             started.append(copy)
     srecv[me_s] = ssend[...]
     precv[me_s] = psend[:, slot_rows(own), :]
-
-    for k in range(1, n_exp):
-        other = partner(me_e, k, n_exp)
-        piece = router_half(other, core)
-        remote(piece, piece, rz_send.at[k], rz_recv.at[k], me_s, other).wait_recv()
-        copy = remote(piece, piece, rs_send.at[k], rs_recv.at[k], sib, me_e)
-        copy.start()
-        started.append(copy)
-    for k in range(1, n_exp):
-        piece = router_half(partner(me_e, k, n_exp), 1 - core)
-        remote(piece, piece, rs_send.at[k], rs_recv.at[k], sib, me_e).wait_recv()
-    for s in range(seqs):
-        mine = tok[s, pl.ds(pl.multiple_of(me_e * rows, rows), rows), :]
-        score = jnp.concatenate(
-            [jnp.dot(mine, routers[e], preferred_element_type=F32) for e in range(n_exp)], axis=1
-        )
-        weight = jnp.exp(score - jnp.max(score, axis=1, keepdims=True))
-        inv[s] = jnp.broadcast_to(1.0 / jnp.sum(weight, axis=1, keepdims=True), (rows, 128))
-        comb[s] = weight.astype(BF16)
 
     for k in range(1, n_seq):
         other = partner(me_s, k, n_seq)
@@ -164,12 +163,15 @@
         act = jax.nn.gelu(pre, approximate=True).astype(BF16)
         result = result + jnp.dot(act, w2[at : at + block, :], preferred_element_type=F32)
 
-    def place(exp, seq):
-        return slots.at[seq % split, :, slot_rows(exp * experts + seq // split), :]
+    def chip_rows(at):
+        return pl.ds(pl.multiple_of(at * SLOTS, SLOTS), SLOTS)
+
+    def place(first, last, at):
+        return slots.at[core, :, first:last, chip_rows(at), :]
 
     part = width // split
     if split == 1:
-        slots[0, :, slot_rows(me_e * experts + own), :] = result.reshape(seqs, SLOTS, width).astype(BF16)
+        slots[core, :, 0, chip_rows(chip), :] = result.reshape(seqs, SLOTS, width).astype(BF16)
     else:
         for q in range(split):
             pout[q] = result[:, q * part : (q + 1) * part].reshape(seqs, SLOTS, part).astype(BF16)
@@ -182,46 +184,86 @@
         for k in range(1, split):
             remote(pout.at[me_q], xrecv.at[k], q_send.at[k], q_recv.at[k], me_s, me_e).wait_recv()
             total = total + xrecv[k].astype(F32)
-        slots[me_q, :, slot_rows(me_e * experts + own), :] = total.astype(BF16)
-
-    for k in range(1, n_exp):
-        piece = place(me_e, me_s)
-        copy = remote(piece, piece, z_send.at[k], z_recv.at[k], me_s, partner(me_e, k, n_exp))
-        copy.start()
-        started.append(copy)
-    for j in range(n_exp):
-        exp = partner(me_e, j, n_exp) if j else me_e
-        piece = place(exp, me_s)
-        if j:
-            remote(piece, piece, z_send.at[j], z_recv.at[j], me_s, exp).wait_recv()
+        slots[core, :, 0, chip_rows(chip), :] = total.astype(BF16)
+
+    groups = [(k, k + 1) for k in range(n_exp)]
+
+    def over(k):
+        return remote(
+            place(0, 1, chip), place(k, k + 1, chip), z_send.at[k], z_recv.at[k], me_s, partner(me_e, k, n_exp)
+        )
+
+    def across(g, k):
+        piece = place(*groups[g], chip)
+        return remote(piece, piece, c_send.at[g, k], c_recv.at[g, k], partner(chip, k, chips) * 2 + core, me_e)
+
+    def across_in(g, k):
+        piece = place(*groups[g], partner(chip, k, chips))
+        return remote(piece, piece, c_send.at[g, k], c_recv.at[g, k], me_s, me_e)
+
+    def share(g, which):
+        first, last = groups[g]
+        piece = slots.at[which, :, first:last, :, :]
+        return remote(piece, piece, b_send.at[g], b_recv.at[g], sib, me_e)
+
+    for k in range(1, n_exp):
+        over(k).start()
+        started.append(over(k))
+    for k in range(1, chips):
+        across(0, k).start()
+        started.append(across(0, k))
+    for k in range(1, n_exp):
+        router_over(k).wait_recv()
+        router_share(k, core).start()
+        started.append(router_share(k, core))
+    for g in range(1, len(groups)):
+        for k in range(*groups[g]):
+            over(k).wait_recv()
         for k in range(1, chips):
-            copy = remote(piece, piece, c_send.at[j, k], c_recv.at[j, k], partner(chip, k, chips) * 2 + core, me_e)
-            copy.start()
-            started.append(copy)
-        copy = remote(piece, piece, b_send.at[j, 0], b_recv.at[j, 0], sib, me_e)
-        copy.start()
-        started.append(copy)
-    for j in range(n_exp):
-        exp = partner(me_e, j, n_exp) if j else me_e
+            across(g, k).start()
+            started.append(across(g, k))
+    for k in range(1, n_exp):
+        router_share(k, 1 - core).wait_recv()
+    for s in range(seqs):
+        mine = tok[s, pl.ds(pl.multiple_of(me_e * rows, rows), rows), :]
+        score = jnp.concatenate(
+            [jnp.dot(mine, routers[e], preferred_element_type=F32) for e in range(n_exp)], axis=1
+        )
+        weight = jnp.exp(score - jnp.max(score, axis=1, keepdims=True))
+        inv[s] = jnp.broadcast_to(1.0 / jnp.sum(weight, axis=1, keepdims=True), (rows, 128))
+        weight = weight.astype(BF16)
+        if split == 1:
+            weight = jnp.dot(weight, perm[...], preferred_element_type=F32).astype(BF16)
+        comb[s] = weight
+
+
+    for g in range(len(groups)):
         for k in range(1, chips):
-            seq = partner(chip, k, chips) * 2 + core
-            piece = place(exp, seq)
-            remote(piece, piece, c_send.at[j, k], c_recv.at[j, k], seq, me_e).wait_recv()
-            copy = remote(piece, piece, b_send.at[j, k], b_recv.at[j, k], sib, me_e)
-            copy.start()
-            started.append(copy)
-    for j in range(n_exp):
-        exp = partner(me_e, j, n_exp) if j else me_e
-        for k in range(chips):
-            seq = (partner(chip, k, chips) if k else chip) * 2 + 1 - core
-            piece = place(exp, seq)
-            remote(piece, piece, b_send.at[j, k], b_recv.at[j, k], sib, me_e).wait_recv()
+            across_in(g, k).wait_recv()
+        share(g, core).start()
+        started.append(share(g, core))
+    for g in range(len(groups)):
+        share(g, 1 - core).wait_recv()
 
     for s in range(seqs):
         scale = inv[s][:, 0:1]
-        for q in range(split):
-            mix = jnp.dot(comb[s], slots[q, s], preferred_element_type=F32) * scale
-            mixed_ref[s, :, q * part : (q + 1) * part] = mix.astype(BF16)
+        if split == 1:
+            side = n_exp * cols // 2
+            mix = jnp.zeros((rows, width), F32)
+            for c in range(2):
+                mix = mix + jnp.dot(
+                    comb[s, :, c * side : (c + 1) * side], slots[c, s].reshape(side, width),
+                    preferred_element_type=F32,
+                )
+            mixed_ref[s] = (mix * scale).astype(BF16)
+        else:
+            sub = split // 2
+            for q in range(split):
+                piece = slots[q % 2, s].reshape(n_exp, chips // sub, sub, SLOTS, part)[:, :, q // 2]
+                mix = jnp.dot(
+                    comb[s], piece.reshape(n_exp * cols, part), preferred_element_type=F32
+                )
+                mixed_ref[s, :, q * part : (q + 1) * part] = (mix * scale).astype(BF16)
 
     for copy in started:
         copy.wait_send()
@@ -257,16 +299,17 @@
             pltpu.VMEM((seqs * SLOTS, width), BF16),
             pltpu.VMEM((split, seqs, SLOTS, part), BF16),
             pltpu.VMEM((split, seqs, SLOTS, part), BF16),
-            pltpu.VMEM((split, seqs, n_exp * cols, part), BF16),
+            pltpu.VMEM((2, seqs, n_exp, chips * SLOTS, part), BF16),
             pltpu.VMEM((seqs, rows, n_exp * cols), BF16),
             pltpu.VMEM((seqs, rows, 128), F32),
+            pltpu.VMEM((n_exp * cols,) * 2 if split == 1 else (16, 128), BF16),
             dma((4,)),
             dma((n_exp,)), dma((n_exp,)), dma((n_exp,)), dma((n_exp,)),
             dma((n_seq,)), dma((n_seq,)), dma((n_seq,)), dma((n_seq,)),
             dma((split,)), dma((split,)),
             dma((n_exp,)), dma((n_exp,)),
             dma((n_exp, chips)), dma((n_exp, chips)),
-            dma((n_exp, chips)), dma((n_exp, chips)),
+            dma((n_exp,)), dma((n_exp,)),
         ],
         compiler_params=pltpu.CompilerParams(
             collective_id=0, has_side_effects=True, vmem_limit_bytes=56 * 1024 * 1024

time: 42.8 us -> 37.6 us (0.88)
  Pallas kernels: 40.1 us -> 35.1 us
    pallas_call x1, Pallas kernels: 40.1 us -> 35.1 us  [shards(): pl.pallas_call(functools.partial(layer, n_seq, n_exp), out_shape=jax.Shap...]
where the time goes in v3:
time: 37.6 us; the launch traced here: 37 us
  Pallas kernels  35.1 us (93%)
  local copies, waits for them, and re-layouts  1.87 us (5%)
    pallas_call x1, Pallas kernels, shards(): pl.pallas_call(functools.partial(layer, n_seq, n_exp), out_shape=jax.Shap...  35.1 us
    unnamed x1, local copies, waits for them, and re-layouts  1.87 us

profile of v3, /device:TPU:0, one launch (start us, length us, event | category | flops | bytes accessed | tf_op | source)
XLA Modules:
  0.0 37.0 jit_solution(3174256276237325011)
XLA Ops:
  0.0 35.1 %shard_map.46 = bf16[2,128,1024]{2,1,0:T(8,128)(2,1)} custom-call(bf16[2,512,1024]{2,1,0:T(8,128)(2,1)} %tokens_ref.1, bf16[1024,128]{1,0:T(8,128)(2,1)} %router_ref.1, bf16[1,1024,2048]{2,1,0:T(8,128)(2,1)} %w_in_ref.1, bf16[1,2048,1024]{2,1,0:T(8,128)(2,1)} %w_out_ref.1), custom_call_target="tpu_custom_call" | custom-call | tf_op jit(solution)/shard_map/pallas_call | solution.py:284
  35.1 1.9 %copy.6 = bf16[2,128,1024]{2,1,0:T(8,128)(2,1)} copy(bf16[2,128,1024]{2,1,0:T(8,128)(2,1)} %shard_map.46) | data formatting | bytes 1048576

commit v4 on v3

--- a/solution.py
+++ b/solution.py
@@ -106,6 +106,20 @@
     loads[1].wait()
     loads[2].start()
     loads[3].start()
+    def slot_rows(expert):
+        return pl.ds(pl.multiple_of(expert * SLOTS, SLOTS), SLOTS)
+
+    def partial(s, k):
+        other = partner(me_s, k, n_seq)
+        return remote(
+            psend.at[s, slot_rows(other // split), :], precv.at[me_s, s], p_send.at[s, k], p_recv.at[s, k], other, me_e
+        )
+
+    def partial_in(s, k):
+        other = partner(me_s, k, n_seq)
+        return remote(psend.at[s, slot_rows(own), :], precv.at[other, s], p_send.at[s, k], p_recv.at[s, k], other, me_e)
+
+    order = [k for k in range(2, n_seq)] + [1]
     ssend[...] = jnp.zeros_like(ssend)
     for s in range(seqs):
         score = jnp.dot(tok[s], routers[0], preferred_element_type=F32)
@@ -114,18 +128,13 @@
         ssend[s : s + 1, :] = top
         ssend[seqs + s : seqs + s + 1, :] = jnp.sum(weight, axis=0, keepdims=True)
         psend[s] = jnp.dot(weight.T.astype(BF16), tok[s], preferred_element_type=F32).astype(BF16)
-
-    def slot_rows(expert):
-        return pl.ds(pl.multiple_of(expert * SLOTS, SLOTS), SLOTS)
-
-    for k in range(1, n_seq):
-        other = partner(me_s, k, n_seq)
-        for copy in (
-            remote(ssend, srecv.at[me_s], s_send.at[k], s_recv.at[k], other, me_e),
-            remote(psend.at[:, slot_rows(other // split), :], precv.at[me_s], p_send.at[k], p_recv.at[k], other, me_e),
-        ):
-            copy.start()
-            started.append(copy)
+        for k in order:
+            partial(s, k).start()
+            started.append(partial(s, k))
+    for k in order:
+        copy = remote(ssend, srecv.at[me_s], s_send.at[k], s_recv.at[k], partner(me_s, k, n_seq), me_e)
+        copy.start()
+        started.append(copy)
     srecv[me_s] = ssend[...]
     precv[me_s] = psend[:, slot_rows(own), :]
 
@@ -143,10 +152,9 @@
         parts.append(jnp.zeros((fill, cols), F32))
     coef[...] = jnp.concatenate(parts, axis=0).T
     factor = coef[slot_rows(own), :]
-    for k in range(1, n_seq):
-        other = partner(me_s, k, n_seq)
-        remote(psend.at[:, slot_rows(own), :], precv.at[other], p_send.at[k], p_recv.at[k], other, me_e).wait_recv()
-    for s in range(seqs):
+    for s in range(seqs):
+        for k in range(1, n_seq):
+            partial_in(s, k).wait_recv()
         total = jnp.zeros((SLOTS, width), F32)
         for i in range(n_seq):
             at = s * n_seq + i
@@ -188,9 +196,13 @@
 
     groups = [(k, k + 1) for k in range(n_exp)]
 
-    def over(k):
+    bits = [1 << b for b in range(n_exp.bit_length() - 1)]
+
+    def over(low, bit):
+        k = low + bit
         return remote(
-            place(0, 1, chip), place(k, k + 1, chip), z_send.at[k], z_recv.at[k], me_s, partner(me_e, k, n_exp)
+            place(low, low + 1, chip), place(k, k + 1, chip), z_send.at[k], z_recv.at[k],
+            me_s, partner(me_e, bit, n_exp),
         )
 
     def across(g, k):
@@ -206,9 +218,9 @@
         piece = slots.at[which, :, first:last, :, :]
         return remote(piece, piece, b_send.at[g], b_recv.at[g], sib, me_e)
 
-    for k in range(1, n_exp):
-        over(k).start()
-        started.append(over(k))
+    for bit in bits:
+        over(0, bit).start()
+        started.append(over(0, bit))
     for k in range(1, chips):
         across(0, k).start()
         started.append(across(0, k))
@@ -217,8 +229,12 @@
         router_share(k, core).start()
         started.append(router_share(k, core))
     for g in range(1, len(groups)):
-        for k in range(*groups[g]):
-            over(k).wait_recv()
+        top = max(bit for bit in bits if bit <= g)
+        over(g - top, top).wait_recv()
+        for bit in bits:
+            if bit > g:
+                over(g, bit).start()
+                started.append(over(g, bit))
         for k in range(1, chips):
             across(g, k).start()
             started.append(across(g, k))
@@ -305,7 +321,7 @@
             pltpu.VMEM((n_exp * cols,) * 2 if split == 1 else (16, 128), BF16),
             dma((4,)),
             dma((n_exp,)), dma((n_exp,)), dma((n_exp,)), dma((n_exp,)),
-            dma((n_seq,)), dma((n_seq,)), dma((n_seq,)), dma((n_seq,)),
+            dma((seqs, n_seq)), dma((seqs, n_seq)), dma((n_seq,)), dma((n_seq,)),
             dma((split,)), dma((split,)),
             dma((n_exp,)), dma((n_exp,)),
             dma((n_exp, chips)), dma((n_exp, chips)),

time: 37.6 us -> 36.4 us (0.968)
  Pallas kernels: 35.1 us -> 33.9 us
    pallas_call x1, Pallas kernels: 35.1 us -> 33.9 us  [shards(): pl.pallas_call(functools.partial(layer, n_seq, n_exp), out_shape=jax.Shap...]
where the time goes in v4:
time: 36.4 us; the launch traced here: 35.8 us
  Pallas kernels  33.9 us (93%)
  local copies, waits for them, and re-layouts  1.87 us (5%)
    pallas_call x1, Pallas kernels, shards(): pl.pallas_call(functools.partial(layer, n_seq, n_exp), out_shape=jax.Shap...  33.9 us
    unnamed x1, local copies, waits for them, and re-layouts  1.87 us

profile of v4, /device:TPU:0, one launch (start us, length us, event | category | flops | bytes accessed | tf_op | source)
XLA Modules:
  0.0 35.8 jit_solution(11342032935480349329)
XLA Ops:
  0.0 33.9 %shard_map.46 = bf16[2,128,1024]{2,1,0:T(8,128)(2,1)} custom-call(bf16[2,512,1024]{2,1,0:T(8,128)(2,1)} %tokens_ref.1, bf16[1024,128]{1,0:T(8,128)(2,1)} %router_ref.1, bf16[1,1024,2048]{2,1,0:T(8,128)(2,1)} %w_in_ref.1, bf16[1,2048,1024]{2,1,0:T(8,128)(2,1)} %w_out_ref.1), custom_call_target="tpu_custom_call" | custom-call | tf_op jit(solution)/shard_map/pallas_call | solution.py:300
  33.9 1.9 %copy.6 = bf16[2,128,1024]{2,1,0:T(8,128)(2,1)} copy(bf16[2,128,1024]{2,1,0:T(8,128)(2,1)} %shard_map.46) | data formatting | bytes 1048576
